TPU v7x, 32 devices: a whole 2x2x4 slice. The times are simulated.
32 devices in a mesh: outer: 4 (over z), inner: 8 (over y, x, core).
Axes of the slice: x: 2, y: 2, z: 4, core: 2. Of those that a mesh axis runs over, the one named last changes fastest.
Arguments:
- tiles: bfloat16 [4096, 128, 128], P(('outer', 'inner')), as said below
- tile_row: int32 [4096], P(('outer', 'inner')), may hold values from 0 to 3, as said below
- tile_col: int32 [4096], P(('outer', 'inner')), may hold values from 0 to 3, as said below
- counts: int32 [1024], P(('outer', 'inner')), may hold values from 1 to 4, as said below
- vectors: bfloat16 [16384, 64], P(('outer', 'inner')), may hold values from -6 to 6
Outputs:
- basis: float32 [16384, 64], P(('outer', 'inner'))
- degree: float32 [16384], P(('outer', 'inner'))
Inputs may be any that keep to these rules, and one draw needn't show every extreme that they name: Slot s from sender g to destination h is live exactly when s < counts[g * 32 + h]; the tiles of dead slots hold values that are no part of P. counts is 4 from every sender to itself and 1 to 4 from every sender to every other destination. `tile_row`: A slot from a sender to itself with number s lies in block row s % 4. `tile_col`: A slot from a sender to itself with number s lies in block column s % 4. `tiles`: entries are affinities, zero or positive.
All inputs are finite; a program needn't handle non-finite values.
Results may differ from a plain program's by a relative error of at most 0.004.
Values may be sent and summed in bfloat16 or wider, within the bound.
A program may use at most 192 MiB of HBM per device.

v0:
```python
import jax
import jax.numpy as jnp
from jax import lax
from jax.sharding import PartitionSpec as P


def shards(tiles, tile_row, tile_col, counts, vectors):
    peer_count = lax.axis_size(("outer", "inner"))
    slot_count = tiles.shape[0] // peer_count
    tile_size = tiles.shape[1]
    rows_dev = vectors.shape[0]
    block_count = rows_dev // tile_size
    vec_width = vectors.shape[1]
    highest = lax.Precision.HIGHEST
    got_tiles, got_rows, got_cols, got_counts = (
        lax.all_to_all(tiles, ("outer", "inner"), split_axis=0, concat_axis=0, tiled=True),
        lax.all_to_all(tile_row, ("outer", "inner"), split_axis=0, concat_axis=0, tiled=True),
        lax.all_to_all(tile_col, ("outer", "inner"), split_axis=0, concat_axis=0, tiled=True),
        lax.all_to_all(counts, ("outer", "inner"), split_axis=0, concat_axis=0, tiled=True),
    )
    got_sums = jnp.sum(got_tiles, axis=1, dtype=jnp.float32)
    slot_number = jnp.arange(slot_count, dtype=jnp.int32)[None, :]
    own_live = (slot_number < counts[:, None]).reshape(-1).astype(jnp.float32)
    got_live = (slot_number < got_counts[:, None]).reshape(-1).astype(jnp.float32)
    block_ids = jnp.arange(block_count, dtype=jnp.int32)[None, :]
    own_weight = (tile_row[:, None] == block_ids).astype(jnp.float32) * own_live[:, None]
    got_weight = (got_cols[:, None] == block_ids).astype(jnp.float32) * got_live[:, None]
    own_sums = jnp.sum(tiles, axis=2, dtype=jnp.float32)
    degree_blocks = jnp.einsum("tr,ta->ra", own_weight, own_sums, precision=highest)
    degree_blocks = degree_blocks + jnp.einsum("tr,ta->ra", got_weight, got_sums, precision=highest)
    degree = 1.0 + degree_blocks.reshape(rows_dev)
    inv_root = lax.rsqrt(degree)
    scaled = (inv_root[:, None] * vectors.astype(jnp.float32)).astype(jnp.bfloat16)

    def piece_layout(piece, start):
        piece_devs = piece.shape[0] // rows_dev
        first_dev = start // rows_dev
        block_vec = piece.reshape(piece_devs, block_count, tile_size, vec_width)
        source_idx = jnp.repeat(jnp.arange(piece_devs, dtype=jnp.int32), slot_count)
        return (block_vec, source_idx, first_dev * slot_count, piece_devs * slot_count)

    empty = jnp.zeros((block_count, tile_size, vec_width), jnp.float32)
    group_vec = lax.all_gather(scaled, "inner", axis=0, tiled=True)
    piece = lax.all_gather(group_vec, "outer", axis=0, tiled=True)
    start = jnp.int32(0)
    block_vec, source_idx, begin, length = piece_layout(piece, start)
    forward = jnp.einsum(
        "tab,tbk->tak", tiles, block_vec[source_idx, tile_col], preferred_element_type=jnp.float32
    )
    block_vec, source_idx, begin, length = piece_layout(piece, start)
    got_mix = got_weight.astype(jnp.bfloat16)
    mirrored = jnp.einsum(
        "tba,tbk->tak",
        got_tiles,
        block_vec[source_idx, got_rows],
        preferred_element_type=jnp.float32,
    )
    total = jnp.einsum("tr,tak->rak", own_weight, forward, precision=highest) + jnp.einsum(
        "tr,tak->rak", got_mix, mirrored.astype(jnp.bfloat16), preferred_element_type=jnp.float32
    )
    total = total + empty
    image = inv_root[:, None] * (total.reshape(rows_dev, vec_width) + scaled.astype(jnp.float32))
    local_gram = jnp.dot(image.T, image, precision=highest)
    gram = lax.psum(local_gram, ("outer", "inner")) / jnp.float32(rows_dev * peer_count)
    lower = jnp.linalg.cholesky(gram)
    basis = jax.scipy.linalg.solve_triangular(lower, image.T, lower=True).T
    return (basis, degree)


def solution(mesh):
    placed = (
        P(("outer", "inner"), None, None),
        P(("outer", "inner")),
        P(("outer", "inner")),
        P(("outer", "inner")),
        P(("outer", "inner"), None),
    )
    return jax.shard_map(
        shards,
        mesh=mesh,
        in_specs=placed,
        out_specs=(P(("outer", "inner"), None), P(("outer", "inner"))),
        check_vma=False,
    )
```

profile of v0, /device:TPU:0, one launch (start us, length us, event | category | flops | bytes accessed | tf_op | source)
XLA Modules:
  0.0 276.4 jit_solution(15112734025049565781)
XLA Ops:
  7.2 1.3 copy.27
  8.5 7.3 %all-to-all-start.1 = ((s32[32,1,1]{2,1,0:T(1,128)}), s32[32,1,1]{2,1,0:T(1,128)S(1)}, u32[]{:S(2)}, u32[]{:S(2)}) async-start(s32[32,1,1]{2,1,0:T(1,128)} %copy.27), calls=%async_computation.1 | async-start | bytes 32768 | tf_op jit(solution)/shard_map/all_to_all | solution.py:19
  15.8 0.8 all_to_all.23
  16.6 6.3 %all-to-all-done.1 = s32[32,1,1]{2,1,0:T(1,128)S(1)} async-done(((s32[32,1,1]{2,1,0:T(1,128)}), s32[32,1,1]{2,1,0:T(1,128)S(1)}, u32[]{:S(2)}, u32[]{:S(2)}) %all-to-all-start.1) | async-done | bytes 160 | tf_op jit(solution)/shard_map/all_to_all | solution.py:19
  22.9 8.8 %all_to_all.35 = s32[32,4,1]{1,2,0:T(1,128)S(1)} all-to-all(s32[32,4,1]{1,2,0:T(1,128)S(1)} %bitcast.55), channel_id=1, replica_groups=mesh['outer'=4,'inner'=8] {'outer','inner'}, dimensions={0} | all-to-all | bytes 1024 | tf_op jit(solution)/shard_map/all_to_all | solution.py:18
  31.7 3.7 %all-to-all-start.2 = ((bf16[128,128,128]{2,1,0:T(8,128)(2,1)}), bf16[128,128,128]{2,1,0:T(8,128)(2,1)}, u32[]{:S(2)}, u32[]{:S(2)}) async-start(bf16[128,128,128]{2,1,0:T(8,128)(2,1)} %param.5), calls=%async_computation.2 | async-start | bytes 8388608 | tf_op jit(solution)/shard_map/all_to_all | solution.py:16
  35.4 0.0 copy-start.2
  35.4 0.0 all-gather.2.cloned.1.call-start
  35.5 0.1 fusion.19
  35.6 0.1 reshape.139
  35.7 0.0 copy-start.1
  35.7 0.0 copy-start.4
  35.7 3.4 %convert_reduce_fusion.1 = f32[128,128]{1,0:T(8,128)S(1)} fusion(bf16[128,128,128]{2,1,0:T(8,128)(2,1)} %param.5), kind=kLoop, calls=%fused_computation.3 | loop fusion | flops 4177920 | bytes 4259840 | tf_op jit(solution)/shard_map/reduce_sum | solution.py:28
  39.1 0.2 fusion.22
  39.3 0.7 reduce.7
  39.9 0.1 fusion.20
  40.0 0.1 reshape.140
  40.1 0.6 broadcast.195
  40.7 0.7 reduce.13
  41.5 0.1 eq.31
  41.6 87.9 %all-to-all-done.2 = bf16[128,128,128]{2,1,0:T(8,128)(2,1)} async-done(((bf16[128,128,128]{2,1,0:T(8,128)(2,1)}), bf16[128,128,128]{2,1,0:T(8,128)(2,1)}, u32[]{:S(2)}, u32[]{:S(2)}) %all-to-all-start.2) | async-done | bytes 4194336 | tf_op jit(solution)/shard_map/all_to_all | solution.py:16
  129.4 3.4 %convert_reduce_fusion = f32[128,128]{1,0:T(8,128)S(1)} fusion(bf16[128,128,128]{2,1,0:T(8,128)(2,1)} %all-to-all-done.2), kind=kLoop, calls=%fused_computation.2 | loop fusion | flops 4177920 | bytes 4259840 | tf_op jit(solution)/shard_map/reduce_sum | solution.py:21
  132.8 0.8 fusion.53
  133.6 10.8 %all_gather.6 = bf16[4096,64]{0,1:T(8,128)(2,1)} all-gather(bf16[512,64]{0,1:T(8,128)(2,1)S(1)} %multiply_convert_fusion), channel_id=1, replica_groups=mesh['outer'=4,'inner'=8] {'inner'}, dimensions={0}, use_global_device_ids=true | all-gather | bytes 589824 | tf_op jit(solution)/shard_map/all_gather | solution.py:43
  144.4 0.0 all-gather.2.cloned.1.call-update
  144.5 0.7 all_to_all.28
  145.2 3.0 %all-to-all-start.3 = ((s32[32,4,1]{1,2,0:T(1,128)}), s32[32,4,1]{1,2,0:T(1,128)S(1)}, u32[]{:S(2)}, u32[]{:S(2)}) async-start(s32[32,4,1]{1,2,0:T(1,128)} %bitcast.8), calls=%async_computation.3 | async-start | bytes 32768 | tf_op jit(solution)/shard_map/all_to_all | solution.py:17
  148.2 0.1 reshape.137
  148.3 7.0 %all-to-all-done.3 = s32[32,4,1]{1,2,0:T(1,128)S(1)} async-done(((s32[32,4,1]{1,2,0:T(1,128)}), s32[32,4,1]{1,2,0:T(1,128)S(1)}, u32[]{:S(2)}, u32[]{:S(2)}) %all-to-all-start.3) | async-done | bytes 544 | tf_op jit(solution)/shard_map/all_to_all | solution.py:17
  155.2 0.7 reduce.14
  156.0 0.1 all_to_all.30
  156.1 32.9 %all-gather.2.cloned.1.call-done = bf16[16384,64]{0,1:T(8,128)(2,1)} async-done(((bf16[4096,64]{0,1:T(8,128)(2,1)}), bf16[16384,64]{0,1:T(8,128)(2,1)}) %all-gather.2.cloned.1.call-update) | async-done | bytes 2097168 | tf_op jit(solution)/shard_map/all_gather | solution.py:44
  189.0 4.5 %reshape.136 = bf16[32,4,128,64]{2,1,0,3:T(4,128)(2,1)} reshape(bf16[16384,64]{0,1:T(8,128)(2,1)} %all-gather.2.cloned.1.call-done) | data formatting | bytes 4194304 | tf_op jit(solution)/shard_map/reshape | solution.py:38
  193.4 4.0 %copy.28 = bf16[32,4,128,64]{2,3,1,0:T(8,128)(2,1)S(1)} copy(bf16[32,4,128,64]{2,1,0,3:T(4,128)(2,1)} %reshape.136) | data formatting | bytes 4194304 | tf_op jit(solution)/shard_map/reshape | solution.py:38
  197.5 2.3 gather_fusion.1
  199.7 2.3 gather_fusion
  202.0 5.8 %convolution_bitcast_fusion = f32[128,128,64]{1,2,0:T(8,128)S(1)} fusion(bf16[128,128,64]{1,2,0:T(8,128)(2,1)} %gather_fusion, bf16[128,128,128]{2,1,0:T(8,128)(2,1)} %param.5), kind=kOutput, calls=%fused_computation.6 | convolution fusion | flops 268435456 | bytes 10485760 | tf_op jit(solution)/shard_map/tab,tbk->tak/dot_general | solution.py:47
  207.8 4.3 %fusion = f32[4,128,64]{1,0,2:T(4,128)S(1)} fusion(f32[128,128,64]{1,2,0:T(8,128)S(1)} %convolution_bitcast_fusion, f32[128]{0:T(128)S(1)} %reshape.139, s32[128]{0:T(128)S(1)} %copy-done.2), kind=kOutput, calls=%fused_computation.4 | convolution fusion | flops 50332672 | bytes 4326400 | tf_op jit(solution)/shard_map/tr,tak->rak/dot_general | solution.py:58
  212.2 3.4 %convert_bitcast_fusion = bf16[128,128,64]{1,2,0:T(8,128)(2,1)S(1)} fusion(bf16[128,128,64]{1,2,0:T(8,128)(2,1)S(1)} %copy-done, bf16[128,128,128]{2,1,0:T(8,128)(2,1)} %all-to-all-done.2), kind=kOutput, calls=%fused_computation.9 | convolution fusion | flops 269484032 | bytes 8388608 | tf_op jit(solution)/shard_map/tba,tbk->tak/dot_general | solution.py:52
  215.6 1.2 fusion.4
  216.8 0.3 fusion.12
  217.1 39.2 %psum.7 = f32[64,64]{0,1:T(8,128)S(1)} all-reduce(f32[64,64]{0,1:T(8,128)S(1)} %fusion.12), channel_id=1, replica_groups=mesh['outer'=4,'inner'=8] {'outer','inner'}, use_global_device_ids=true, to_apply=%region_2.0 | all-reduce | flops 4096 | bytes 32768 | tf_op jit(solution)/shard_map/psum | solution.py:64
  256.4 0.1 copy.34
  256.4 5.8 %cholesky.16 = f32[64,64]{1,0:T(8,128)S(1)} custom-call(f32[64,64]{1,0:T(8,128)S(1)} %fusion.18), custom_call_target="Cholesky" | custom-call | tf_op jit(solution)/shard_map/jit(cholesky)/cholesky | solution.py:65
  262.3 0.6 compare_reduce_fusion
  263.0 0.7 fusion.16
  263.6 4.9 %custom-call.7 = f32[1,64,64]{1,2,0:T(8,128)S(1)} custom-call(f32[1,64,64]{2,1,0:T(8,128)S(1)} %fusion.16), custom_call_target="InvertDiagBlocksLowerTriangular" | custom-call | tf_op jit(solution)/shard_map/jit(_solve_triangular)/triangular_solve | solution.py:66
  268.5 1.0 fusion.10
  (13 shorter events, 0.1 us)
Async XLA Ops:
  8.5 14.4 %all-to-all-start.1 = ((s32[32,1,1]{2,1,0:T(1,128)}), s32[32,1,1]{2,1,0:T(1,128)S(1)}, u32[]{:S(2)}, u32[]{:S(2)}) async-start(s32[32,1,1]{2,1,0:T(1,128)} %copy.27), calls=%async_computation.1 | async-start | bytes 32768 | tf_op jit(solution)/shard_map/all_to_all | solution.py:19
  31.7 3.8 %copy-start.3 = (s32[32]{0:T(128)S(1)}, s32[32]{0:T(128)}, u32[]{:S(2)}) copy-start(s32[32]{0:T(128)} %param.8) | copy-start | bytes 388
  31.7 97.7 %all-to-all-start.2 = ((bf16[128,128,128]{2,1,0:T(8,128)(2,1)}), bf16[128,128,128]{2,1,0:T(8,128)(2,1)}, u32[]{:S(2)}, u32[]{:S(2)}) async-start(bf16[128,128,128]{2,1,0:T(8,128)(2,1)} %param.5), calls=%async_computation.2 | async-start | bytes 8388608 | tf_op jit(solution)/shard_map/all_to_all | solution.py:16
  35.4 3.7 %copy-start.2 = (s32[128]{0:T(128)S(1)}, s32[128]{0:T(128)}, u32[]{:S(2)}) copy-start(s32[128]{0:T(128)} %param.6) | copy-start | bytes 1540
  35.4 153.5 %all-gather.2.cloned.1.call-start = ((), (), s32[]{:S(2)}) async-start(), calls=%async_computation.4 | async-start | bytes 2621440 | tf_op jit(solution)/shard_map/all_gather | solution.py:44
  35.7 97.9 %copy-start.1 = (bf16[512,64]{0,1:T(8,128)(2,1)S(1)}, bf16[512,64]{0,1:T(8,128)(2,1)}, u32[]{:S(2)}) copy-start(bf16[512,64]{0,1:T(8,128)(2,1)} %param.9) | copy-start | bytes 196612
  35.7 120.4 %copy-start.4 = (s32[128]{0:T(128)S(1)}, s32[128]{0:T(128)}, u32[]{:S(2)}) copy-start(s32[128]{0:T(128)} %param.7) | copy-start | bytes 1540
  145.2 10.1 %all-to-all-start.3 = ((s32[32,4,1]{1,2,0:T(1,128)}), s32[32,4,1]{1,2,0:T(1,128)S(1)}, u32[]{:S(2)}, u32[]{:S(2)}) async-start(s32[32,4,1]{1,2,0:T(1,128)} %bitcast.8), calls=%async_computation.3 | async-start | bytes 32768 | tf_op jit(solution)/shard_map/all_to_all | solution.py:17
  207.8 4.4 %copy-start = (bf16[128,128,64]{1,2,0:T(8,128)(2,1)S(1)}, bf16[128,128,64]{1,2,0:T(8,128)(2,1)}, u32[]{:S(2)}) copy-start(bf16[128,128,64]{1,2,0:T(8,128)(2,1)} %gather_fusion.1) | copy-start | bytes 6291460
Sparse Core Ops, SparseCore 0:
  144.6 44.3 all-gather.1
where the time goes:
time: 277 us; the launch traced here: 276 us
  waiting for transfers between devices  134 us (48%)
  blocking collectives  58.9 us (21%)
  other arithmetic  21.2 us (8%)
  local copies, waits for them, and re-layouts  17.1 us (6%)
  matrix products  16.9 us (6%)
  between operations  14.2 us (5%)
  starting transfers between devices  14 us (5%)
    all_to_all x1, waiting for transfers between devices, shards(): lax.all_to_all(tiles, ('outer', 'inner'), split_axis=0, concat_axis=0, ti...  87.9 us
    psum x1, blocking collectives, shards(): lax.psum(local_gram, ('outer', 'inner'))  39.2 us
    all_gather x1, waiting for transfers between devices, shards(): piece = lax.all_gather(group_vec, 'outer', axis=0, tiled=True)  32.9 us
    all_gather x1, blocking collectives, shards(): group_vec = lax.all_gather(scaled, 'inner', axis=0, tiled=True)  10.8 us
    all_to_all x1, blocking collectives, shards(): lax.all_to_all(tile_col, ('outer', 'inner'), split_axis=0, concat_axis=0,...  8.83 us
    reshape x2, local copies, waits for them, and re-layouts, piece_layout(): block_vec = piece.reshape(piece_devs, block_count, tile_size, vec_width)  8.49 us
    all_to_all x1, starting transfers between devices, shards(): lax.all_to_all(counts, ('outer', 'inner'), split_axis=0, concat_axis=0, t...  7.3 us
    all_to_all x1, waiting for transfers between devices, shards(): lax.all_to_all(tile_row, ('outer', 'inner'), split_axis=0, concat_axis=0,...  6.95 us
  transfers between devices with their start and end apart: 4, of which 4 were waited for; matrix products, arithmetic and copies ran while one was open for 2% of the time, Pallas kernels for 0%

commit v1 on v0

v1 whole, which is shorter than its diff:
```python
import functools

import jax
import jax.numpy as jnp
from jax import lax
from jax.experimental import pallas as pl
from jax.experimental.pallas import tpu as pltpu
from jax.sharding import PartitionSpec as P

MESH = pl.DeviceIdType.MESH
BF = jnp.bfloat16
F32 = jnp.float32
NT = (((1,), (1,)), ((), ()))
HI = lax.Precision.HIGHEST


def exchange(
    no, ni, ns, nb, k, ts,
    row_ref, col_ref, cnt_ref, tiles_hbm, v_ref,
    img_ref, deg_ref, gram_ref,
    tiles, vall, csum, crecv, invall, own, mout, rcore, asum, rplane, bsum, rz, fwd, ginner, gz,
    tile_sem, vz_s, vz_r, vp_s, vp_r, vc_s, vc_r, cs_s, cs_r, iv_s, iv_r,
    rc_s, rc_r, rp_s, rp_r, rz_s, rz_r, g1_s, g1_r, g2_s, g2_r,
):
    nc = ni // 2
    n = no * ni
    z = lax.axis_index("outer")
    i = lax.axis_index("inner")
    me = z * ni + i
    chip = i // 2
    core = i % 2
    sib = chip * 2 + (1 - core)

    def zof(d):
        return lax.rem(z + d, no)

    def cof(d):
        return lax.rem(chip + d, nc)

    def iof(d):
        return lax.rem(i + d, ni)

    def hof(d):
        return lax.rem(me + d, n)

    def loop(lo, hi, body):
        def step(j, carry):
            body(j)
            return carry
        lax.fori_loop(lo, hi, step, 0)

    def remote(src, dst, ssem, rsem, zz, ii):
        return pltpu.make_async_remote_copy(
            src_ref=src, dst_ref=dst, send_sem=ssem, recv_sem=rsem,
            device_id=(zz, ii), device_id_type=MESH)

    def tile_copy(q):
        part = pl.ds(q * ni, ni)
        return pltpu.make_async_copy(tiles_hbm.at[part], tiles.at[part], tile_sem.at[q])

    for q in range(no):
        tile_copy(q).start()

    barrier = pltpu.get_barrier_semaphore()

    def greet(d):
        h = hof(d)
        pl.semaphore_signal(barrier, inc=1, device_id=(h // ni, h % ni), device_id_type=MESH)
    loop(1, n, greet)
    pl.semaphore_wait(barrier, n - 1)

    def vz(d):
        return remote(v_ref, vall.at[me], vz_s.at[d], vz_r.at[z], zof(d), i)

    def vz_in(d):
        zz = zof(d)
        return remote(v_ref, vall.at[zz * ni + i], vz_s.at[d], vz_r.at[zz], zz, i)

    def vp(zd, d):
        zz = zof(zd)
        slot = vall.at[zz * ni + i]
        return remote(slot, slot, vp_s.at[zd, d], vp_r.at[zz, chip], z, cof(d) * 2 + core)

    def vp_in(zd, d):
        zz, cc = zof(zd), cof(d)
        slot = vall.at[zz * ni + cc * 2 + core]
        return remote(slot, slot, vp_s.at[zd, d], vp_r.at[zz, cc], z, cc * 2 + core)

    def vc(zd, d):
        zz, cc = zof(zd), cof(d)
        slot = vall.at[zz * ni + cc * 2 + core]
        return remote(slot, slot, vc_s.at[zd, d], vc_r.at[zz, cc], z, sib)

    def vc_in(zd, d):
        zz, cc = zof(zd), cof(d)
        slot = vall.at[zz * ni + cc * 2 + (1 - core)]
        return remote(slot, slot, vc_s.at[zd, d], vc_r.at[zz, cc], z, sib)

    vall[me] = v_ref[...]
    loop(1, no, lambda d: vz(d).start())
    loop(1, nc, lambda d: vp(0, d).start())
    vc(0, 0).start()

    iota8 = lax.broadcasted_iota(jnp.int32, (8, ts), 0)

    def live_index(ref, h, s):
        return jnp.where(s < cnt_ref[h], ref[h * ns + s], -1)

    def sums(h, racc):
        t = tiles[h]
        wc = jnp.concatenate(
            [jnp.where(iota8 == live_index(col_ref, h, s), 1.0, 0.0).astype(BF) for s in range(ns)], axis=1)
        csum[h] = jnp.dot(wc, t, preferred_element_type=F32)[:nb]
        for s in range(ns):
            wr = jnp.where(iota8 == live_index(row_ref, h, s), 1.0, 0.0).astype(BF)
            racc = racc + lax.dot_general(wr, t[s * ts:(s + 1) * ts], NT, preferred_element_type=F32)
        return racc

    racc = jnp.zeros((8, ts), F32)
    for q in range(no):
        tile_copy(q).wait()
        racc = lax.fori_loop(q * ni, (q + 1) * ni, sums, racc)

    def cs(d):
        h = hof(d)
        return remote(csum.at[h], crecv.at[me], cs_s.at[d], cs_r.at[me], h // ni, h % ni)

    def cs_in(d):
        h = hof(d)
        return remote(csum.at[h], crecv.at[h], cs_s.at[d], cs_r.at[h], h // ni, h % ni)

    loop(1, n, lambda d: cs(d).start())

    def relay_z(zd):
        vz_in(zd).wait_recv()
        loop(1, nc, lambda d: vp(zd, d).start())
        vc(zd, 0).start()
    loop(1, no, relay_z)

    def add_sums(d, acc):
        cs_in(d).wait_recv()
        return acc + crecv[hof(d)]
    degree = lax.fori_loop(1, n, add_sums, 1.0 + racc[:nb] + csum[me])
    deg_ref[...] = degree
    invall[me] = lax.rsqrt(degree)

    def iv(d):
        h = hof(d)
        return remote(invall.at[me], invall.at[me], iv_s.at[d], iv_r.at[me], h // ni, h % ni)

    def iv_in(d):
        h = hof(d)
        return remote(invall.at[h], invall.at[h], iv_s.at[d], iv_r.at[h], h // ni, h % ni)

    loop(1, n, lambda d: iv(d).start())

    inv = invall[me]
    for b in range(nb):
        own[b] = (inv[b:b + 1] * v_ref[b].astype(F32)).astype(BF).astype(F32)

    def mirror(zz, cc, half):
        h = zz * ni + cc * 2 + half
        parts = [[] for _ in range(nb)]
        for s in range(ns):
            c = live_index(col_ref, h, s)
            rows = own[row_ref[h * ns + s]]
            for b in range(nb):
                parts[b].append((rows * jnp.where(c == b, 1.0, 0.0)).astype(BF))
        left = jnp.concatenate([jnp.concatenate(p, axis=1) for p in parts], axis=0)
        m = jnp.dot(left, tiles[h], preferred_element_type=F32)
        mout[half, zz, cc] = m.astype(BF).reshape(nb, k, ts)

    def rc(zd):
        zz = zof(zd)
        return remote(mout.at[1 - core, zz], rcore.at[zz], rc_s.at[zz], rc_r.at[zz], z, sib)

    def rp(zd, d):
        zz, cc = zof(zd), cof(d)
        return remote(asum.at[zz, cc], rplane.at[zz, chip], rp_s.at[zd, d], rp_r.at[zz, chip], z, cc * 2 + core)

    def rp_in(zd, d):
        zz, cc = zof(zd), cof(d)
        return remote(asum.at[zz, cc], rplane.at[zz, cc], rp_s.at[zd, d], rp_r.at[zz, cc], z, cc * 2 + core)

    def rzc(zd):
        return remote(bsum.at[zof(zd)], rz.at[z], rz_s.at[zd], rz_r.at[z], zof(zd), i)

    def rz_in(zd):
        zz = zof(zd)
        return remote(bsum.at[zz], rz.at[zz], rz_s.at[zd], rz_r.at[zz], zz, i)

    def make_chunk(zo):
        zd = lax.rem(zo + 1, no)
        zz = zof(zd)
        loop(0, nc, lambda cc: mirror(zz, cc, 1 - core))
        rc(zd).start()
        loop(0, nc, lambda cc: mirror(zz, cc, core))
    loop(0, no, make_chunk)

    def send_chunk(zo):
        zd = lax.rem(zo + 1, no)
        zz = zof(zd)
        rc(zd).wait_recv()

        def add_one(d):
            cc = cof(d)
            asum[zz, cc] = (mout[core, zz, cc].astype(F32) + rcore[zz, cc].astype(F32)).astype(BF)

        def add_send(d):
            add_one(d)
            rp(zd, d).start()
        loop(1, nc, add_send)
        add_one(0)
    loop(0, no, send_chunk)

    def relay_p(zd):
        def one(d):
            vp_in(zd, d).wait_recv()
            vc(zd, d).start()
        loop(1, nc, one)
    loop(0, no, relay_p)
    loop(1, n, lambda d: iv_in(d).wait_recv())
    loop(0, no, lambda zd: loop(0, nc, lambda d: vc_in(zd, d).wait_recv()))

    fwd[...] = jnp.zeros_like(fwd)

    def forward(h):
        acc = fwd[...]
        for s in range(ns):
            c = col_ref[h * ns + s]
            r = live_index(row_ref, h, s)
            blk = (inv_row(h, c) * vall[h, c].astype(F32)).astype(BF).astype(F32)
            left = jnp.concatenate([(blk * jnp.where(r == b, 1.0, 0.0)).astype(BF) for b in range(nb)], axis=0)
            acc = acc + lax.dot_general(left, tiles[h, s * ts:(s + 1) * ts], NT, preferred_element_type=F32)
        fwd[...] = acc

    def inv_row(h, c):
        rows = invall[h]
        out = rows[0:1]
        for b in range(1, nb):
            out = jnp.where(jnp.broadcast_to(c, out.shape) == b, rows[b:b + 1], out)
        return out

    def work(zo):
        zd = lax.rem(zo + 1, no)
        zz = zof(zd)
        loop(zz * ni, (zz + 1) * ni, forward)
        total = asum[zz, chip].astype(F32)

        def add_p(d, acc):
            rp_in(zd, d).wait_recv()
            return acc + rplane[zz, cof(d)].astype(F32)
        total = lax.fori_loop(1, nc, add_p, total)
        bsum[zz] = total.astype(BF)

    def work_send(zo):
        work(zo)
        rzc(lax.rem(zo + 1, no)).start()
    loop(0, no - 1, work_send)
    work(no - 1)

    def add_z(d, acc):
        rz_in(d).wait_recv()
        return acc + rz[zof(d)].astype(F32)
    total = lax.fori_loop(1, no, add_z, bsum[z].astype(F32))
    gram = jnp.zeros((k, k), F32)
    for b in range(nb):
        x = inv[b:b + 1] * (total[b] + fwd[b * k:(b + 1) * k] + own[b])
        img_ref[b] = x
        gram = gram + lax.dot_general(x, x, NT, preferred_element_type=F32, precision=HI)
    half = k // 2
    ginner[i] = jnp.concatenate([gram[:half], gram[half:]], axis=1)

    def g1(d):
        return remote(ginner.at[i], ginner.at[i], g1_s.at[d], g1_r.at[i], z, iof(d))

    def g1_in(d):
        ii = iof(d)
        return remote(ginner.at[ii], ginner.at[ii], g1_s.at[d], g1_r.at[ii], z, ii)

    def g2(d):
        return remote(gz.at[z], gz.at[z], g2_s.at[d], g2_r.at[z], zof(d), i)

    def g2_in(d):
        zz = zof(d)
        return remote(gz.at[zz], gz.at[zz], g2_s.at[d], g2_r.at[zz], zz, i)

    loop(1, ni, lambda d: g1(d).start())
    loop(1, ni, lambda d: g1_in(d).wait_recv())
    gz[z] = lax.fori_loop(1, ni, lambda j, a: a + ginner[j], ginner[0])
    loop(1, no, lambda d: g2(d).start())
    loop(1, no, lambda d: g2_in(d).wait_recv())
    g = lax.fori_loop(1, no, lambda j, a: a + gz[j], gz[0])
    gram_ref[...] = g * (1.0 / (n * nb * ts))

    loop(1, no, lambda d: vz(d).wait_send())
    loop(0, no, lambda zd: loop(1, nc, lambda d: vp(zd, d).wait_send()))
    loop(0, no, lambda zd: loop(0, nc, lambda d: vc(zd, d).wait_send()))
    loop(1, n, lambda d: cs(d).wait_send())
    loop(1, n, lambda d: iv(d).wait_send())
    loop(0, no, lambda zd: rc(zd).wait_send())
    loop(0, no, lambda zd: loop(1, nc, lambda d: rp(zd, d).wait_send()))
    loop(1, no, lambda zd: rzc(zd).wait_send())
    loop(1, ni, lambda d: g1(d).wait_send())
    loop(1, no, lambda d: g2(d).wait_send())


def orthonormalize(k, gram_ref, img_ref, out_ref):
    g = gram_ref[...]
    a = jnp.concatenate([g[:, :k], g[:, k:]], axis=0)
    row = lax.broadcasted_iota(jnp.int32, (k, k), 0)
    col = lax.broadcasted_iota(jnp.int32, (k, k), 1)
    a = jnp.concatenate([a, jnp.where(row == col, 1.0, 0.0)], axis=1)
    rows = lax.broadcasted_iota(jnp.int32, (k, 2 * k), 0)
    scale = jnp.zeros((k, 2 * k), F32)
    for j in range(k):
        c = jnp.broadcast_to(a[:, j:j + 1], (k, 2 * k))
        piv = c[j:j + 1]
        scale = jnp.where(rows == j, c, scale)
        a = a - jnp.where(rows > j, c, 0.0) * (a[j:j + 1] / piv)
    inv_low = (a * lax.rsqrt(scale))[:, k:]
    for b in range(img_ref.shape[0]):
        ts = img_ref.shape[2]
        out_ref[b * ts:(b + 1) * ts, :] = lax.dot_general(
            img_ref[b], inv_low, (((0,), (1,)), ((), ())), preferred_element_type=F32, precision=HI)


def shards(tiles, tile_row, tile_col, counts, vectors):
    no, ni = lax.axis_size("outer"), lax.axis_size("inner")
    n = no * ni
    nc = ni // 2
    ns = tiles.shape[0] // n
    ts = tiles.shape[1]
    k = vectors.shape[1]
    nb = vectors.shape[0] // ts
    vt = jnp.swapaxes(vectors.reshape(nb, ts, k), 1, 2)
    dma = pltpu.SemaphoreType.DMA
    blk = (nb, k, ts)
    vmem = pl.BlockSpec(memory_space=pltpu.VMEM)
    smem = pl.BlockSpec(memory_space=pltpu.SMEM)
    img, deg, gram = pl.pallas_call(
        functools.partial(exchange, no, ni, ns, nb, k, ts),
        out_shape=(
            jax.ShapeDtypeStruct(blk, F32),
            jax.ShapeDtypeStruct((nb, ts), F32),
            jax.ShapeDtypeStruct((k // 2, 2 * k), F32),
        ),
        in_specs=[smem, smem, smem, pl.BlockSpec(memory_space=pl.ANY), vmem],
        out_specs=(vmem, vmem, vmem),
        scratch_shapes=[
            pltpu.VMEM((n, ns * ts, ts), BF),
            pltpu.VMEM((n,) + blk, BF),
            pltpu.VMEM((n, nb, ts), F32),
            pltpu.VMEM((n, nb, ts), F32),
            pltpu.VMEM((n, nb, ts), F32),
            pltpu.VMEM(blk, F32),
            pltpu.VMEM((2, no, nc) + blk, BF),
            pltpu.VMEM((no, nc) + blk, BF),
            pltpu.VMEM((no, nc) + blk, BF),
            pltpu.VMEM((no, nc) + blk, BF),
            pltpu.VMEM((no,) + blk, BF),
            pltpu.VMEM((no,) + blk, BF),
            pltpu.VMEM((nb * k, ts), F32),
            pltpu.VMEM((ni, k // 2, 2 * k), F32),
            pltpu.VMEM((no, k // 2, 2 * k), F32),
            dma((no,)),
            dma((no,)), dma((no,)),
            dma((no, nc)), dma((no, nc)),
            dma((no, nc)), dma((no, nc)),
            dma((n,)), dma((n,)),
            dma((n,)), dma((n,)),
            dma((no,)), dma((no,)),
            dma((no, nc)), dma((no, nc)),
            dma((no,)), dma((no,)),
            dma((ni,)), dma((ni,)),
            dma((no,)), dma((no,)),
        ],
        compiler_params=pltpu.CompilerParams(
            collective_id=0, has_side_effects=True, vmem_limit_bytes=60 * 2**20),
        name="exchange",
    )(tile_row, tile_col, counts, tiles.reshape(n, ns * ts, ts), vt)
    basis = pl.pallas_call(
        functools.partial(orthonormalize, k),
        out_shape=jax.ShapeDtypeStruct((nb * ts, k), F32),
        in_specs=[vmem, vmem],
        out_specs=vmem,
        name="orthonormalize",
    )(gram, img)
    return (basis, deg.reshape(nb * ts))


def solution(mesh):
    placed = (
        P(("outer", "inner"), None, None),
        P(("outer", "inner")),
        P(("outer", "inner")),
        P(("outer", "inner")),
        P(("outer", "inner"), None),
    )
    return jax.shard_map(
        shards,
        mesh=mesh,
        in_specs=placed,
        out_specs=(P(("outer", "inner"), None), P(("outer", "inner"))),
        check_vma=False,
    )
```

time: 277 us -> 66 us (0.24)
  waiting for transfers between devices: 134 us -> 0 us
  Pallas kernels: 0 us -> 60.6 us
  blocking collectives: 58.9 us -> 0 us
  other arithmetic: 21.2 us -> 0 us
  matrix products: 16.9 us -> 0 us
  starting transfers between devices: 14 us -> 0 us
  between operations: 14.2 us -> 0.65 us
  local copies, waits for them, and re-layouts: 17.1 us -> 4.44 us
    all_to_all x3 -> x0, waiting for transfers between devices: 101 us -> none  [the longest x1 87.9 us: shards(): lax.all_to_all(tiles, ('outer', 'inner'), split_axis=0, concat_axis=0, ti...]
    pallas_call x0 -> x2, Pallas kernels: none -> 60.6 us  [the longest x1 53.2 us: shards(): pl.pallas_call(functools.partial(exchange, no, ni, ns, nb, k, ts), out_sh...]
    psum x1 -> x0, blocking collectives: 39.2 us -> none  [shards(): lax.psum(local_gram, ('outer', 'inner'))]
    all_gather x1 -> x0, waiting for transfers between devices: 32.9 us -> none  [shards(): piece = lax.all_gather(group_vec, 'outer', axis=0, tiled=True)]
    dot_general x7 -> x0, matrix products: 16 us -> none  [the longest x1 5.79 us: shards(): jnp.einsum('tab,tbk->tak', tiles, block_vec[source_idx, tile_col], prefer...]
    all_to_all x3 -> x0, starting transfers between devices: 14 us -> none  [the longest x1 7.3 us: shards(): lax.all_to_all(counts, ('outer', 'inner'), split_axis=0, concat_axis=0, t...]
    another operation x5 -> x0, other arithmetic: 12.1 us -> none  [the longest x3 6.52 us: shards(): lower = jnp.linalg.cholesky(gram)]
    all_gather x1 -> x0, blocking collectives: 10.8 us -> none  [shards(): group_vec = lax.all_gather(scaled, 'inner', axis=0, tiled=True)]
  transfers between devices with their start and end apart: 4 -> 0, of which waited for: 4 -> 0; matrix products, arithmetic and copies ran while one was open for 2% -> 0% of each run, Pallas kernels for 0% -> 0%
where the time goes in v1:
time: 66 us; the launch traced here: 65.7 us
  Pallas kernels  60.6 us (92%)
  local copies, waits for them, and re-layouts  4.44 us (7%)
    pallas_call x1, Pallas kernels, shards(): pl.pallas_call(functools.partial(exchange, no, ni, ns, nb, k, ts), out_sh...  53.2 us
    pallas_call x1, Pallas kernels, shards(): pl.pallas_call(functools.partial(orthonormalize, k), out_shape=jax.ShapeD...  7.44 us
    unnamed x4, local copies, waits for them, and re-layouts  3.8 us

profile of v1, /device:TPU:0, one launch (start us, length us, event | category | flops | bytes accessed | tf_op | source)
XLA Modules:
  0.0 65.7 jit_solution(15316182981053468094)
XLA Ops:
  0.6 0.0 copy-start
  0.6 0.8 %copy-done = bf16[512,64]{0,1:T(8,128)(2,1)S(1)} copy-done((bf16[512,64]{0,1:T(8,128)(2,1)S(1)}, bf16[512,64]{0,1:T(8,128)(2,1)}, u32[]{:S(2)}) %copy-start) | copy-done | bytes 65560
  1.5 0.6 bitcast_bitcast_fusion.v_ref
  2.1 53.2 %exchange.1 = (f32[4,64,128]{2,1,0:T(8,128)}, f32[4,128]{1,0:T(4,128)}, f32[32,128]{1,0:T(8,128)}) custom-call(s32[128]{0:T(128)} %row_ref.1, s32[128]{0:T(128)} %col_ref.1, s32[32]{0:T(128)} %cnt_ref.1, bf16[32,512,128]{2,1,0:T(8,128)(2,1)} %bitcast.9, bf16[4,64,128]{2,1,0:T(8,128)(2,1)} %bitcast_bitcast_fusion.v_ref), custom_call_target="tpu_custom_call" | custom-call | tf_op jit(solution)/shard_map/exchange/pallas_call | solution.py:341
  55.3 7.4 %orthonormalize.1 = f32[512,64]{1,0:T(8,128)} custom-call(f32[32,128]{1,0:T(8,128)} %get-tuple-element.5.gram_ref, f32[4,64,128]{2,1,0:T(8,128)} %get-tuple-element.6.img_ref), custom_call_target="tpu_custom_call" | custom-call | tf_op jit(solution)/shard_map/orthonormalize/pallas_call | solution.py:382
  62.7 1.7 %copy.9 = f32[512,64]{0,1:T(8,128)} copy(f32[512,64]{1,0:T(8,128)} %orthonormalize.1) | data formatting | bytes 262144
  64.4 1.2 %copy.13 = f32[512]{0:T(512)} copy(f32[512]{0:T(512)} %bitcast.10) | data formatting | bytes 4096
Async XLA Ops:
  0.6 0.8 %copy-start = (bf16[512,64]{0,1:T(8,128)(2,1)S(1)}, bf16[512,64]{0,1:T(8,128)(2,1)}, u32[]{:S(2)}) copy-start(bf16[512,64]{0,1:T(8,128)(2,1)} %param.9) | copy-start | bytes 196612

commit v2 on v1

--- a/solution.py
+++ b/solution.py
@@ -70,11 +70,11 @@
     pl.semaphore_wait(barrier, n - 1)
 
     def vz(d):
-        return remote(v_ref, vall.at[me], vz_s.at[d], vz_r.at[z], zof(d), i)
+        return remote(vall.at[me], vall.at[me], vz_s.at[d], vz_r.at[z], zof(d), i)
 
     def vz_in(d):
         zz = zof(d)
-        return remote(v_ref, vall.at[zz * ni + i], vz_s.at[d], vz_r.at[zz], zz, i)
+        return remote(vall.at[me], vall.at[zz * ni + i], vz_s.at[d], vz_r.at[zz], zz, i)
 
     def vp(zd, d):
         zz = zof(zd)
@@ -96,10 +96,8 @@
         slot = vall.at[zz * ni + cc * 2 + (1 - core)]
         return remote(slot, slot, vc_s.at[zd, d], vc_r.at[zz, cc], z, sib)
 
-    vall[me] = v_ref[...]
-    loop(1, no, lambda d: vz(d).start())
-    loop(1, nc, lambda d: vp(0, d).start())
-    vc(0, 0).start()
+    for b in range(nb):
+        vall[me, b] = v_ref[:, b * ts:(b + 1) * ts]
 
     iota8 = lax.broadcasted_iota(jnp.int32, (8, ts), 0)
 
@@ -131,11 +129,9 @@
 
     loop(1, n, lambda d: cs(d).start())
 
-    def relay_z(zd):
-        vz_in(zd).wait_recv()
-        loop(1, nc, lambda d: vp(zd, d).start())
-        vc(zd, 0).start()
-    loop(1, no, relay_z)
+    loop(1, no, lambda d: vz(d).start())
+    loop(1, nc, lambda d: vp(0, d).start())
+    vc(0, 0).start()
 
     def add_sums(d, acc):
         cs_in(d).wait_recv()
@@ -156,7 +152,7 @@
 
     inv = invall[me]
     for b in range(nb):
-        own[b] = (inv[b:b + 1] * v_ref[b].astype(F32)).astype(BF).astype(F32)
+        own[b] = (inv[b:b + 1] * vall[me, b].astype(F32)).astype(BF).astype(F32)
 
     def mirror(zz, cc, half):
         h = zz * ni + cc * 2 + half
@@ -197,6 +193,12 @@
         loop(0, nc, lambda cc: mirror(zz, cc, core))
     loop(0, no, make_chunk)
 
+    def relay_z(zd):
+        vz_in(zd).wait_recv()
+        loop(1, nc, lambda d: vp(zd, d).start())
+        vc(zd, 0).start()
+    loop(1, no, relay_z)
+
     def send_chunk(zo):
         zd = lax.rem(zo + 1, no)
         zz = zof(zd)
@@ -305,7 +307,8 @@
     loop(1, no, lambda d: g2(d).wait_send())
 
 
-def orthonormalize(k, gram_ref, img_ref, out_ref):
+def orthonormalize(k, gram_ref, img_ref, deg_ref, out_ref, deg_out):
+    deg_out[...] = deg_ref[...]
     g = gram_ref[...]
     a = jnp.concatenate([g[:, :k], g[:, k:]], axis=0)
     row = lax.broadcasted_iota(jnp.int32, (k, k), 0)
@@ -321,8 +324,8 @@
     inv_low = (a * lax.rsqrt(scale))[:, k:]
     for b in range(img_ref.shape[0]):
         ts = img_ref.shape[2]
-        out_ref[b * ts:(b + 1) * ts, :] = lax.dot_general(
-            img_ref[b], inv_low, (((0,), (1,)), ((), ())), preferred_element_type=F32, precision=HI)
+        out_ref[:, b * ts:(b + 1) * ts] = jnp.dot(
+            inv_low, img_ref[b], preferred_element_type=F32, precision=HI)
 
 
 def shards(tiles, tile_row, tile_col, counts, vectors):
@@ -333,7 +336,6 @@
     ts = tiles.shape[1]
     k = vectors.shape[1]
     nb = vectors.shape[0] // ts
-    vt = jnp.swapaxes(vectors.reshape(nb, ts, k), 1, 2)
     dma = pltpu.SemaphoreType.DMA
     blk = (nb, k, ts)
     vmem = pl.BlockSpec(memory_space=pltpu.VMEM)
@@ -378,15 +380,18 @@
         compiler_params=pltpu.CompilerParams(
             collective_id=0, has_side_effects=True, vmem_limit_bytes=60 * 2**20),
         name="exchange",
-    )(tile_row, tile_col, counts, tiles.reshape(n, ns * ts, ts), vt)
-    basis = pl.pallas_call(
+    )(tile_row, tile_col, counts, tiles.reshape(n, ns * ts, ts), vectors.T)
+    basis, deg = pl.pallas_call(
         functools.partial(orthonormalize, k),
-        out_shape=jax.ShapeDtypeStruct((nb * ts, k), F32),
-        in_specs=[vmem, vmem],
-        out_specs=vmem,
+        out_shape=(
+            jax.ShapeDtypeStruct((k, nb * ts), F32),
+            jax.ShapeDtypeStruct((nb, ts), F32),
+        ),
+        in_specs=[vmem, vmem, vmem],
+        out_specs=(vmem, vmem),
         name="orthonormalize",
-    )(gram, img)
-    return (basis, deg.reshape(nb * ts))
+    )(gram, img, deg)
+    return (basis.T, deg.reshape(nb * ts))
 
 
 def solution(mesh):

time: 66 us -> 71.6 us (1.085)
  Pallas kernels: 60.6 us -> 70.8 us
  local copies, waits for them, and re-layouts: 4.44 us -> 0 us
    pallas_call x1, Pallas kernels: 53.2 us -> 63.6 us  [shards(): pl.pallas_call(functools.partial(exchange, no, ni, ns, nb, k, ts), out_sh...]
    unnamed x4 -> x0, local copies, waits for them, and re-layouts: 3.8 us -> none
where the time goes in v2:
time: 71.6 us; the launch traced here: 71.5 us
  Pallas kernels  70.8 us (99%)
    pallas_call x1, Pallas kernels, shards(): pl.pallas_call(functools.partial(exchange, no, ni, ns, nb, k, ts), out_sh...  63.6 us
    pallas_call x1, Pallas kernels, shards(): pl.pallas_call(functools.partial(orthonormalize, k), out_shape=(jax.Shape...  7.26 us

profile of v2, /device:TPU:0, one launch (start us, length us, event | category | flops | bytes accessed | tf_op | source)
XLA Modules:
  0.0 71.5 jit_solution(17437073288152782399)
XLA Ops:
  0.6 63.6 %exchange.1 = (f32[4,64,128]{2,1,0:T(8,128)}, f32[4,128]{1,0:T(4,128)}, f32[32,128]{1,0:T(8,128)}) custom-call(s32[128]{0:T(128)} %row_ref.1, s32[128]{0:T(128)} %col_ref.1, s32[32]{0:T(128)} %cnt_ref.1, bf16[32,512,128]{2,1,0:T(8,128)(2,1)} %bitcast.4, bf16[64,512]{1,0:T(8,128)(2,1)} %bitcast.5), custom_call_target="tpu_custom_call" | custom-call | tf_op jit(solution)/shard_map/exchange/pallas_call | solution.py:343
  64.2 7.3 %orthonormalize.1 = (f32[64,512]{1,0:T(8,128)}, f32[4,128]{1,0:T(4,128)}) custom-call(f32[32,128]{1,0:T(8,128)} %get-tuple-element.7.gram_ref, f32[4,64,128]{2,1,0:T(8,128)} %get-tuple-element.8.img_ref, f32[4,128]{1,0:T(4,128)} %get-tuple-element.9.deg_ref), custom_call_target="tpu_custom_call" | custom-call | tf_op jit(solution)/shard_map/orthonormalize/pallas_call | solution.py:384

commit v3 on v2

--- a/solution.py
+++ b/solution.py
@@ -98,6 +98,9 @@
 
     for b in range(nb):
         vall[me, b] = v_ref[:, b * ts:(b + 1) * ts]
+    loop(1, no, lambda d: vz(d).start())
+    loop(1, nc, lambda d: vp(0, d).start())
+    vc(0, 0).start()
 
     iota8 = lax.broadcasted_iota(jnp.int32, (8, ts), 0)
 
@@ -129,9 +132,11 @@
 
     loop(1, n, lambda d: cs(d).start())
 
-    loop(1, no, lambda d: vz(d).start())
-    loop(1, nc, lambda d: vp(0, d).start())
-    vc(0, 0).start()
+    def relay_z(zd):
+        vz_in(zd).wait_recv()
+        loop(1, nc, lambda d: vp(zd, d).start())
+        vc(zd, 0).start()
+    loop(1, no, relay_z)
 
     def add_sums(d, acc):
         cs_in(d).wait_recv()
@@ -192,12 +197,6 @@
         rc(zd).start()
         loop(0, nc, lambda cc: mirror(zz, cc, core))
     loop(0, no, make_chunk)
-
-    def relay_z(zd):
-        vz_in(zd).wait_recv()
-        loop(1, nc, lambda d: vp(zd, d).start())
-        vc(zd, 0).start()
-    loop(1, no, relay_z)
 
     def send_chunk(zo):
         zd = lax.rem(zo + 1, no)

time: 71.6 us -> 61.3 us (0.86)
  Pallas kernels: 70.8 us -> 60.5 us
    pallas_call x1, Pallas kernels: 63.6 us -> 53.2 us  [shards(): pl.pallas_call(functools.partial(exchange, no, ni, ns, nb, k, ts), out_sh...]
where the time goes in v3:
time: 61.3 us; the launch traced here: 61.1 us
  Pallas kernels  60.5 us (99%)
  between operations  0.64 us (1%)
    pallas_call x1, Pallas kernels, shards(): pl.pallas_call(functools.partial(exchange, no, ni, ns, nb, k, ts), out_sh...  53.2 us
    pallas_call x1, Pallas kernels, shards(): pl.pallas_call(functools.partial(orthonormalize, k), out_shape=(jax.Shape...  7.26 us

profile of v3, /device:TPU:0, one launch (start us, length us, event | category | flops | bytes accessed | tf_op | source)
XLA Modules:
  0.0 61.1 jit_solution(10523670023125829852)
XLA Ops:
  0.6 53.2 %exchange.1 = (f32[4,64,128]{2,1,0:T(8,128)}, f32[4,128]{1,0:T(4,128)}, f32[32,128]{1,0:T(8,128)}) custom-call(s32[128]{0:T(128)} %row_ref.1, s32[128]{0:T(128)} %col_ref.1, s32[32]{0:T(128)} %cnt_ref.1, bf16[32,512,128]{2,1,0:T(8,128)(2,1)} %bitcast.4, bf16[64,512]{1,0:T(8,128)(2,1)} %bitcast.5), custom_call_target="tpu_custom_call" | custom-call | tf_op jit(solution)/shard_map/exchange/pallas_call | solution.py:342
  53.9 7.3 %orthonormalize.1 = (f32[64,512]{1,0:T(8,128)}, f32[4,128]{1,0:T(4,128)}) custom-call(f32[32,128]{1,0:T(8,128)} %get-tuple-element.7.gram_ref, f32[4,64,128]{2,1,0:T(8,128)} %get-tuple-element.8.img_ref, f32[4,128]{1,0:T(4,128)} %get-tuple-element.9.deg_ref), custom_call_target="tpu_custom_call" | custom-call | tf_op jit(solution)/shard_map/orthonormalize/pallas_call | solution.py:383

commit v4 on v3

--- a/solution.py
+++ b/solution.py
@@ -315,11 +315,19 @@
     a = jnp.concatenate([a, jnp.where(row == col, 1.0, 0.0)], axis=1)
     rows = lax.broadcasted_iota(jnp.int32, (k, 2 * k), 0)
     scale = jnp.zeros((k, 2 * k), F32)
-    for j in range(k):
-        c = jnp.broadcast_to(a[:, j:j + 1], (k, 2 * k))
-        piv = c[j:j + 1]
-        scale = jnp.where(rows == j, c, scale)
-        a = a - jnp.where(rows > j, c, 0.0) * (a[j:j + 1] / piv)
+    for j0 in range(0, k, 8):
+        cols = [jnp.broadcast_to(a[:, j0 + q:j0 + q + 1], (k, 2 * k)) for q in range(8)]
+        lines = [a[j0 + q:j0 + q + 1] for q in range(8)]
+        for q in range(8):
+            c, j = cols[q], j0 + q
+            over = 1.0 / c[j:j + 1]
+            line = lines[q] * over
+            scale = jnp.where(rows == j, c, scale)
+            for p in range(q + 1, 8):
+                at = c[j0 + p:j0 + p + 1]
+                lines[p] = lines[p] - at * line
+                cols[p] = cols[p] - c * (at * over)
+            a = a - jnp.where(rows > j, c, 0.0) * line
     inv_low = (a * lax.rsqrt(scale))[:, k:]
     for b in range(img_ref.shape[0]):
         ts = img_ref.shape[2]

time: 61.3 us -> 57.5 us (0.938)
  Pallas kernels: 60.5 us -> 56.7 us
    pallas_call x1, Pallas kernels: 7.26 us -> 3.49 us  [shards(): pl.pallas_call(functools.partial(orthonormalize, k), out_shape=(jax.Shape...]
where the time goes in v4:
time: 57.5 us; the launch traced here: 57.4 us
  Pallas kernels  56.7 us (99%)
  between operations  0.64 us (1%)
    pallas_call x1, Pallas kernels, shards(): pl.pallas_call(functools.partial(exchange, no, ni, ns, nb, k, ts), out_sh...  53.2 us
    pallas_call x1, Pallas kernels, shards(): pl.pallas_call(functools.partial(orthonormalize, k), out_shape=(jax.Shape...  3.49 us

profile of v4, /device:TPU:0, one launch (start us, length us, event | category | flops | bytes accessed | tf_op | source)
XLA Modules:
  0.0 57.4 jit_solution(1225030239584487174)
XLA Ops:
  0.6 53.2 %exchange.1 = (f32[4,64,128]{2,1,0:T(8,128)}, f32[4,128]{1,0:T(4,128)}, f32[32,128]{1,0:T(8,128)}) custom-call(s32[128]{0:T(128)} %row_ref.1, s32[128]{0:T(128)} %col_ref.1, s32[32]{0:T(128)} %cnt_ref.1, bf16[32,512,128]{2,1,0:T(8,128)(2,1)} %bitcast.4, bf16[64,512]{1,0:T(8,128)(2,1)} %bitcast.5), custom_call_target="tpu_custom_call" | custom-call | tf_op jit(solution)/shard_map/exchange/pallas_call | solution.py:350
  53.9 3.5 %orthonormalize.1 = (f32[64,512]{1,0:T(8,128)}, f32[4,128]{1,0:T(4,128)}) custom-call(f32[32,128]{1,0:T(8,128)} %get-tuple-element.7.gram_ref, f32[4,64,128]{2,1,0:T(8,128)} %get-tuple-element.8.img_ref, f32[4,128]{1,0:T(4,128)} %get-tuple-element.9.deg_ref), custom_call_target="tpu_custom_call" | custom-call | tf_op jit(solution)/shard_map/orthonormalize/pallas_call | solution.py:391

commit v5 on v4

--- a/solution.py
+++ b/solution.py
@@ -196,7 +196,6 @@
         loop(0, nc, lambda cc: mirror(zz, cc, 1 - core))
         rc(zd).start()
         loop(0, nc, lambda cc: mirror(zz, cc, core))
-    loop(0, no, make_chunk)
 
     def send_chunk(zo):
         zd = lax.rem(zo + 1, no)
@@ -212,7 +211,13 @@
             rp(zd, d).start()
         loop(1, nc, add_send)
         add_one(0)
-    loop(0, no, send_chunk)
+    make_chunk(0)
+
+    def make_send(zo):
+        make_chunk(zo)
+        send_chunk(zo - 1)
+    loop(1, no, make_send)
+    send_chunk(no - 1)
 
     def relay_p(zd):
         def one(d):

time: 57.5 us -> 55.8 us (0.970)
  Pallas kernels: 56.7 us -> 55 us
    pallas_call x1, Pallas kernels: 53.2 us -> 51.5 us  [shards(): pl.pallas_call(functools.partial(exchange, no, ni, ns, nb, k, ts), out_sh...]
where the time goes in v5:
time: 55.8 us; the launch traced here: 55.7 us
  Pallas kernels  55 us (99%)
  between operations  0.64 us (1%)
    pallas_call x1, Pallas kernels, shards(): pl.pallas_call(functools.partial(exchange, no, ni, ns, nb, k, ts), out_sh...  51.5 us
    pallas_call x1, Pallas kernels, shards(): pl.pallas_call(functools.partial(orthonormalize, k), out_shape=(jax.Shape...  3.5 us

profile of v5, /device:TPU:0, one launch (start us, length us, event | category | flops | bytes accessed | tf_op | source)
XLA Modules:
  0.0 55.7 jit_solution(17053821555823585156)
XLA Ops:
  0.6 51.5 %exchange.1 = (f32[4,64,128]{2,1,0:T(8,128)}, f32[4,128]{1,0:T(4,128)}, f32[32,128]{1,0:T(8,128)}) custom-call(s32[128]{0:T(128)} %row_ref.1, s32[128]{0:T(128)} %col_ref.1, s32[32]{0:T(128)} %cnt_ref.1, bf16[32,512,128]{2,1,0:T(8,128)(2,1)} %bitcast.4, bf16[64,512]{1,0:T(8,128)(2,1)} %bitcast.5), custom_call_target="tpu_custom_call" | custom-call | tf_op jit(solution)/shard_map/exchange/pallas_call | solution.py:355
  52.2 3.5 %orthonormalize.1 = (f32[64,512]{1,0:T(8,128)}, f32[4,128]{1,0:T(4,128)}) custom-call(f32[32,128]{1,0:T(8,128)} %get-tuple-element.7.gram_ref, f32[4,64,128]{2,1,0:T(8,128)} %get-tuple-element.8.img_ref, f32[4,128]{1,0:T(4,128)} %get-tuple-element.9.deg_ref), custom_call_target="tpu_custom_call" | custom-call | tf_op jit(solution)/shard_map/orthonormalize/pallas_call | solution.py:396

commit v6 on v5

--- a/solution.py
+++ b/solution.py
@@ -250,7 +250,6 @@
     def work(zo):
         zd = lax.rem(zo + 1, no)
         zz = zof(zd)
-        loop(zz * ni, (zz + 1) * ni, forward)
         total = asum[zz, chip].astype(F32)
 
         def add_p(d, acc):
@@ -259,11 +258,17 @@
         total = lax.fori_loop(1, nc, add_p, total)
         bsum[zz] = total.astype(BF)
 
+    def forward_chunk(zo):
+        zz = zof(lax.rem(zo + 1, no))
+        loop(zz * ni, (zz + 1) * ni, forward)
+
     def work_send(zo):
         work(zo)
         rzc(lax.rem(zo + 1, no)).start()
+        forward_chunk(zo)
     loop(0, no - 1, work_send)
     work(no - 1)
+    forward_chunk(no - 1)
 
     def add_z(d, acc):
         rz_in(d).wait_recv()
@@ -320,15 +325,15 @@
     a = jnp.concatenate([a, jnp.where(row == col, 1.0, 0.0)], axis=1)
     rows = lax.broadcasted_iota(jnp.int32, (k, 2 * k), 0)
     scale = jnp.zeros((k, 2 * k), F32)
-    for j0 in range(0, k, 8):
-        cols = [jnp.broadcast_to(a[:, j0 + q:j0 + q + 1], (k, 2 * k)) for q in range(8)]
-        lines = [a[j0 + q:j0 + q + 1] for q in range(8)]
-        for q in range(8):
+    for j0 in range(0, k, 16):
+        cols = [jnp.broadcast_to(a[:, j0 + q:j0 + q + 1], (k, 2 * k)) for q in range(16)]
+        lines = [a[j0 + q:j0 + q + 1] for q in range(16)]
+        for q in range(16):
             c, j = cols[q], j0 + q
             over = 1.0 / c[j:j + 1]
             line = lines[q] * over
             scale = jnp.where(rows == j, c, scale)
-            for p in range(q + 1, 8):
+            for p in range(q + 1, 16):
                 at = c[j0 + p:j0 + p + 1]
                 lines[p] = lines[p] - at * line
                 cols[p] = cols[p] - c * (at * over)

time: 55.8 us -> 55.9 us (level)
  no operation moved by 1% of the time
where the time goes in v6:
time: 55.9 us; the launch traced here: 55.7 us
  Pallas kernels  55.1 us (99%)
  between operations  0.64 us (1%)
    pallas_call x1, Pallas kernels, shards(): pl.pallas_call(functools.partial(exchange, no, ni, ns, nb, k, ts), out_sh...  51.5 us
    pallas_call x1, Pallas kernels, shards(): pl.pallas_call(functools.partial(orthonormalize, k), out_shape=(jax.Shape...  3.52 us

profile of v6, /device:TPU:0, one launch (start us, length us, event | category | flops | bytes accessed | tf_op | source)
XLA Modules:
  0.0 55.7 jit_solution(18232972640968631405)
XLA Ops:
  0.6 51.5 %exchange.1 = (f32[4,64,128]{2,1,0:T(8,128)}, f32[4,128]{1,0:T(4,128)}, f32[32,128]{1,0:T(8,128)}) custom-call(s32[128]{0:T(128)} %row_ref.1, s32[128]{0:T(128)} %col_ref.1, s32[32]{0:T(128)} %cnt_ref.1, bf16[32,512,128]{2,1,0:T(8,128)(2,1)} %bitcast.4, bf16[64,512]{1,0:T(8,128)(2,1)} %bitcast.5), custom_call_target="tpu_custom_call" | custom-call | tf_op jit(solution)/shard_map/exchange/pallas_call | solution.py:360
  52.2 3.5 %orthonormalize.1 = (f32[64,512]{1,0:T(8,128)}, f32[4,128]{1,0:T(4,128)}) custom-call(f32[32,128]{1,0:T(8,128)} %get-tuple-element.7.gram_ref, f32[4,64,128]{2,1,0:T(8,128)} %get-tuple-element.8.img_ref, f32[4,128]{1,0:T(4,128)} %get-tuple-element.9.deg_ref), custom_call_target="tpu_custom_call" | custom-call | tf_op jit(solution)/shard_map/orthonormalize/pallas_call | solution.py:401
